TPU v7x, 256 devices: a whole 4x4x8 slice. The times are simulated.
256 devices in a mesh: grp: 8 (over y_lo, x), dom: 32 (over z, y_hi, core).
Axes of the slice: x: 4, y: 4 (y_hi: 2, y_lo: 2; y = y_hi * 2 + y_lo), z: 8, core: 2. Of those that a mesh axis runs over, the one named last changes fastest.
Arguments:
- positions: float32 [3, 16384], P(None, ('grp', 'dom')), may hold values from -6 to 6
- species: int32 [16384], P(('grp', 'dom')), may hold values from 0 to 7
- ghost_index: int32 [2048], P(('grp', 'dom')), may hold values from 0 to 63, as said below
- bin_load: int32 [256], P(('grp', 'dom')), may hold values from 2 to 16, as said below
- neighbour: int32 [4096, 256], P(('grp', 'dom')), may hold values from 0 to 95, as said below
- pair_count: int32 [4096, 4], P(('grp', 'dom')), may hold values from 32 to 64, as said below
- species_shift: float32 [8], replicated, may hold values from -4 to 4
- w_embed1: float32 [256, 24], replicated, may hold values from -5 to 5
- w_embed2: float32 [256, 256], replicated, may hold values from -0.375 to 0.375
- w_v0: float32 [64, 256], replicated, may hold values from -0.375 to 0.375
- w_env: float32 [2, 64, 256], replicated, may hold values from -0.375 to 0.375
- w_lat1: float32 [2, 256, 448], replicated, may hold values from -0.25 to 0.25
- w_lat2: float32 [2, 256, 256], replicated, may hold values from -0.375 to 0.375
- w_gate: float32 [1, 64, 256], replicated, may hold values from -0.375 to 0.375
- w_mix: float32 [1, 3, 64, 64], replicated, may hold values from -0.75 to 0.75
- w_out1: float32 [128, 256], replicated, may hold values from -0.375 to 0.375
- w_out2: float32 [128], replicated, may hold values from -0.5 to 0.5
Outputs:
- forces: float32 [3, 16384], P(None, ('grp', 'dom'))
- atom_energy: float32 [16384], P(('grp', 'dom'))
Inputs may be any that keep to these rules, and one draw needn't show every extreme that they name: `ghost_index`: each device's list names 8 distinct atoms of its occupied bin slots. `bin_load`: the number of occupied bin slots of each device; occupied slots come first. `neighbour`: slots within a center's pair_count never name the center itself nor an own atom of an empty bin slot; other slots hold arbitrary valid indices. `pair_count`: occupied slots of a center are its first ones.
All inputs are finite; a program needn't handle non-finite values.
Results may differ from a plain program's by a relative error of at most 0.0003.
Values sent between devices are 32-bit elements; how exact they have to be, the bound alone decides.
No kernel may reach another device: no remote copies, remote signals or barrier semaphores. Data moves between devices by JAX's collectives and lax.ppermute only.
A program may use at most 128 MiB of HBM per device.

v0:
```python
import math

import jax
import jax.numpy as jnp
from jax import lax
from jax.sharding import PartitionSpec as P

highest = lax.Precision.HIGHEST
soft_sq = 0.25
basis_reach = 8.0
envelope_reach = 4.0
half_root = math.sqrt(0.5)


def extended_2(cells, sides, width):
    for axis, dim in sides:
        count = lax.axis_size(axis)
        head = lax.slice_in_dim(cells, 0, width, axis=dim)
        tail = lax.slice_in_dim(cells, cells.shape[dim] - width, cells.shape[dim], axis=dim)
        cells = jnp.concatenate(
            [
                lax.ppermute(tail, axis, [(i, (i + 1) % count) for i in range(count)]),
                cells,
                lax.ppermute(head, axis, [((i + 1) % count, i) for i in range(count)]),
            ],
            axis=dim,
        )
    return cells


def partner(shard, axis, bit):
    return lax.ppermute(shard, axis, [(i, i ^ 1 << bit) for i in range(lax.axis_size(axis))])


def matmul(left, right):
    return jnp.dot(left, right, precision=highest, preferred_element_type=jnp.float32)


def edge_geometry(offsets, radial):
    dist_sq = jnp.sum(offsets * offsets, axis=0) + soft_sq
    distance = jnp.sqrt(dist_sq)
    unit_x = offsets[0] / distance
    unit_y = offsets[1] / distance
    unit_z = offsets[2] / distance
    root3 = math.sqrt(3.0)
    root5 = math.sqrt(5.0)
    root15 = math.sqrt(15.0)
    harmonics = jnp.stack(
        [
            jnp.ones_like(distance),
            root3 * unit_x,
            root3 * unit_y,
            root3 * unit_z,
            root15 * unit_x * unit_y,
            root15 * unit_y * unit_z,
            0.5 * root5 * (2.0 * unit_z * unit_z - unit_x * unit_x - unit_y * unit_y),
            root15 * unit_x * unit_z,
            0.5 * root15 * (unit_x * unit_x - unit_y * unit_y),
        ]
    )
    scaled = dist_sq / (envelope_reach * envelope_reach)
    envelope = 1.0 / (1.0 + scaled * scaled)
    orders = jnp.arange(1, radial + 1, dtype=jnp.float32)[:, None]
    basis = (
        math.sqrt(2.0 / basis_reach)
        * jnp.sin(orders * (math.pi / basis_reach) * distance[None])
        / distance[None]
        * envelope[None]
    )
    return (harmonics, envelope, basis)


def two_body(offsets, kinds, embed_first, embed_second, tensor_weight):
    harmonics, envelope, basis = edge_geometry(offsets, embed_first.shape[1] - kinds.shape[0])
    inputs = jnp.concatenate([kinds, basis], axis=0)
    latent = envelope[None] * matmul(embed_second, jax.nn.silu(matmul(embed_first, inputs)))
    tensor = matmul(tensor_weight, latent)[None] * harmonics[:, None, :]
    return (latent, tensor, harmonics, envelope)


def interaction(latent, tensor, harmonics, envelope, valid, neigh, layer_weights):
    env_weight, lat_first, lat_second, gate_weight, mix_weight, out_first, out_second = (
        layer_weights
    )
    pairs = harmonics.shape[1]
    centers = pairs // neigh
    channels = env_weight.shape[1]
    layers = env_weight.shape[0]
    for layer in range(layers):
        weight = matmul(env_weight[layer], latent) * valid[None]
        spread = (harmonics[:, None, :] * weight[None]).reshape(9, channels, centers, neigh)
        gamma = jnp.sum(spread, axis=3, keepdims=True) * neigh ** (-0.5)
        gamma = jnp.broadcast_to(gamma, spread.shape).reshape(9, channels, pairs)
        product = tensor * gamma
        scalars = jnp.concatenate(
            [product[0], jnp.sum(product[1:4], axis=0), jnp.sum(product[4:9], axis=0)], axis=0
        )
        hidden = jax.nn.silu(matmul(lat_first[layer], jnp.concatenate([latent, scalars], axis=0)))
        latent = half_root * (latent + envelope[None] * matmul(lat_second[layer], hidden))
        if layer + 1 < layers:
            gate = matmul(gate_weight[layer], latent)
            tensor_zero = tensor[0]
            gamma_zero = gamma[0]
            coupled = tensor_zero[None] * gamma[1:] + gamma_zero[None] * tensor[1:]
            tensor_one = tensor[1:4]
            gamma_one = gamma[1:4]
            cross = jnp.stack(
                [
                    tensor_one[1] * gamma_one[2] - tensor_one[2] * gamma_one[1],
                    tensor_one[2] * gamma_one[0] - tensor_one[0] * gamma_one[2],
                    tensor_one[0] * gamma_one[1] - tensor_one[1] * gamma_one[0],
                ]
            )
            order_zero = (tensor_zero * gamma_zero * gate)[None]
            order_one = (coupled[0:3] + cross) * gate[None]
            order_two = coupled[3:8] * gate[None]
            mixed_zero = jnp.einsum(
                "cd,mdp->mcp", mix_weight[layer, 0], order_zero, precision=highest
            )
            mixed_one = jnp.einsum(
                "cd,mdp->mcp", mix_weight[layer, 1], order_one, precision=highest
            )
            mixed_two = jnp.einsum(
                "cd,mdp->mcp", mix_weight[layer, 2], order_two, precision=highest
            )
            tensor = jnp.concatenate([mixed_zero, mixed_one, mixed_two], axis=0)
    edge = envelope * matmul(out_second[None], jax.nn.silu(matmul(out_first, latent)))[0]
    return jnp.sum((edge * valid).reshape(centers, neigh), axis=1)


def run_blocks(count, worker, inputs, start):

    def step(index, outputs):
        item = tuple(
            (lax.dynamic_index_in_dim(source, index, 0, keepdims=False) for source in inputs)
        )
        results = worker(*item)
        return tuple(
            (
                lax.dynamic_update_index_in_dim(target, result, index, 0)
                for target, result in zip(outputs, results)
            )
        )

    return lax.fori_loop(0, count, step, start)


def local(
    positions,
    species,
    ghost_index,
    bin_load,
    neighbour,
    pair_count,
    species_shift,
    w_embed1,
    w_embed2,
    w_v0,
    w_env,
    w_lat1,
    w_lat2,
    w_gate,
    w_mix,
    w_out1,
    w_out2,
):
    atoms = positions.shape[1]
    bins, pairs = neighbour.shape
    centers = pair_count.shape[1]
    neigh = pairs // centers
    ghosts = ghost_index.shape[0]
    kind_count = species_shift.shape[0]
    load = bin_load[0]
    layer_weights = (w_env, w_lat1, w_lat2, w_gate, w_mix, w_out1, w_out2)
    shell = jnp.concatenate(
        [positions[:, ghost_index], species[ghost_index].astype(jnp.float32)[None]], axis=0
    )
    padded = extended_2(shell[None, None], (("grp", 0), ("dom", 1)), 1)
    received = jnp.concatenate([padded[0, 1], padded[2, 1], padded[1, 0], padded[1, 2]], axis=1)
    extended_pos = jnp.concatenate([positions, received[0:3]], axis=1)
    extended_kind = jnp.concatenate([species, received[3].astype(jnp.int32)], axis=0)
    extended = extended_pos.shape[1]
    center_local = jnp.arange(bins)[:, None] * centers + (jnp.arange(pairs) // neigh)[None, :]
    offsets = jnp.transpose(extended_pos[:, neighbour] - positions[:, center_local], (1, 0, 2))
    center_kind = species[center_local]
    other_kind = extended_kind[neighbour]
    slot = jnp.arange(pairs) % neigh
    valid = (slot[None] < jnp.repeat(pair_count, neigh, axis=1)).astype(jnp.float32)
    kind_range = jnp.arange(kind_count)[None, :, None]
    kinds = jnp.concatenate(
        [center_kind[:, None] == kind_range, other_kind[:, None] == kind_range], axis=1
    ).astype(jnp.float32)

    def full_block(offsets_one, kinds_one, valid_one):

        def energy_of(shifted):
            latent, tensor, harmonics, envelope = two_body(
                shifted, kinds_one, w_embed1, w_embed2, w_v0
            )
            return interaction(latent, tensor, harmonics, envelope, valid_one, neigh, layer_weights)

        energies_one, pull = jax.vjp(energy_of, offsets_one)
        return (energies_one, pull(jnp.ones_like(energies_one))[0])

    def empty_results(count):
        return (jnp.zeros((count, centers), jnp.float32), jnp.zeros((count, 3, pairs), jnp.float32))

    half = bins // 2
    top = lax.axis_size("dom").bit_length() - 1
    bit = top - 1
    upper_live = (jnp.arange(half, bins) < load).astype(jnp.float32)[:, None]
    valid_up = valid[half:] * upper_live
    lower_count = jnp.minimum(load, half)
    packed = jnp.concatenate(
        [
            offsets[half:],
            center_kind[half:, None].astype(jnp.float32),
            other_kind[half:, None].astype(jnp.float32),
            valid_up[:, None],
        ],
        axis=1,
    )
    arrived = partner(packed, "dom", bit)
    energies_low, grads_low = run_blocks(
        lower_count, full_block, (offsets[:half], kinds[:half], valid[:half]), empty_results(half)
    )
    float_range = jnp.arange(kind_count, dtype=jnp.float32)[:, None]

    def remote_block(item):
        kinds_one = jnp.concatenate(
            [item[3][None] == float_range, item[4][None] == float_range], axis=0
        ).astype(jnp.float32)
        return full_block(item[0:3], kinds_one, item[5])

    helped_count = jnp.sum(jnp.max(arrived[:, 5], axis=1) > 0)
    helped = run_blocks(helped_count, remote_block, (arrived,), empty_results(half))
    energies_up, grads_up = partner((helped[0], helped[1]), "dom", bit)
    energies = jnp.concatenate([energies_low, energies_up], axis=0)
    grads = jnp.concatenate([grads_low, grads_up], axis=0)
    center_force = jnp.sum(grads.reshape(bins, 3, centers, neigh), axis=3)
    own_force = jnp.transpose(center_force, (1, 0, 2)).reshape(3, atoms)
    pulled = jnp.transpose(grads, (1, 0, 2)).reshape(3, bins * pairs)
    extended_force = (
        jnp.zeros((3, extended), jnp.float32).at[:, neighbour.reshape(bins * pairs)].add(-pulled)
    )
    force_own = own_force + extended_force[:, :atoms]
    ghost_part = extended_force[:, atoms:].reshape(3, 4, ghosts)
    grp_back = extended_2(jnp.stack([ghost_part[:, 0], ghost_part[:, 1]]), (("grp", 0),), 1)
    dom_back = extended_2(jnp.stack([ghost_part[:, 2], ghost_part[:, 3]]), (("dom", 0),), 1)
    shell_force = grp_back[0] + grp_back[3] + dom_back[0] + dom_back[3]
    forces = force_own.at[:, ghost_index].add(shell_force)
    live_atom = (jnp.arange(atoms) // centers < load).astype(jnp.float32)
    onehot_kind = (species[:, None] == jnp.arange(kind_count)[None, :]).astype(jnp.float32)
    shift = jnp.sum(onehot_kind * species_shift[None, :], axis=1)
    atom_energy = energies.reshape(atoms) + live_atom * shift
    return (forces, atom_energy)


def solution(mesh):
    in_specs = (
        P(None, ("grp", "dom")),
        P(("grp", "dom")),
        P(("grp", "dom")),
        P(("grp", "dom")),
        P(("grp", "dom"), None),
        P(("grp", "dom"), None),
        P(),
        P(),
        P(),
        P(),
        P(),
        P(),
        P(),
        P(),
        P(),
        P(),
        P(),
    )
    out_specs = (P(None, ("grp", "dom")), P(("grp", "dom")))
    return jax.shard_map(local, mesh=mesh, in_specs=in_specs, out_specs=out_specs, check_vma=False)
```

profile of v0, /device:TPU:6, one launch (start us, length us, event | category | flops | bytes accessed | tf_op | source)
XLA Modules:
  0.0 1285.0 jit_solution(14980694010518807113)
XLA Ops:
  5.0 3.3 collective-permute-start
  11.2 24.7 %gather_fusion.4 = s32[4096]{0:T(1024)S(1)} fusion(s32[64]{0:T(128)S(1)} %copy-done, s32[4096]{0:T(1024)S(1)} %broadcast_clamp_fusion), kind=kCustom, calls=%fused_computation.4 | custom fusion | bytes 49152 | tf_op jit(solution)/shard_map/gather | solution.py:185
  38.0 7.4 collective-permute-start.3
  45.5 14.1 %gather_fusion.3 = f32[4096,3]{1,0:T(8,128)} fusion(f32[3,64]{0,1:T(8,128)S(1)} %copy.199, s32[4096]{0:T(1024)S(1)} %broadcast_clamp_fusion), kind=kCustom, calls=%fused_computation.3 | custom fusion | bytes 114688 | tf_op jit(solution)/shard_map/gather | solution.py:184
  60.2 6.7 collective-permute-done.2
  67.0 24.7 %gather_fusion.5 = s32[4096]{0:T(1024)S(1)} fusion(s32[96]{0:T(128)S(1)} %pad_add_fusion.11, s32[4096]{0:T(1024)S(1)} %broadcast_clamp_fusion.1), kind=kCustom, calls=%fused_computation.5 | custom fusion | bytes 49152 | tf_op jit(solution)/shard_map/gather | solution.py:186
  92.5 14.1 %gather_fusion.2 = f32[4096,3]{1,0:T(8,128)} fusion(f32[3,96]{0,1:T(8,128)S(1)} %copy.202, s32[4096]{0:T(1024)S(1)} %broadcast_clamp_fusion.1), kind=kCustom, calls=%fused_computation.2 | custom fusion | bytes 114688 | tf_op jit(solution)/shard_map/gather | solution.py:184
  106.5 2.4 sub.191
  112.2 561.0 %while.26 = (s32[]{:T(128)}, f32[8,4]{1,0:T(8,128)}, f32[8,3,256]{2,1,0:T(4,128)}, s32[]{:T(128)}, f32[8,3,256]{2,1,0:T(4,128)}, /*index=5*/f32[8,16,256]{2,1,0:...) while((s32[]{:T(128)}, f32[8,4]{1,0:T(8,128)}, ...), condition=%wide.region_27.28_spmd, body=%wide.region_0.27_spmd.sunk | while | flops 3500648704 | bytes 109537840 | solution.py:145
  147.3 1.8 fusion.581
  157.1 1.8 broadcast_multiply_fusion.59
  158.9 1.9 broadcast_multiply_fusion.60
  215.3 1.8 fusion.581
  225.1 1.8 broadcast_multiply_fusion.59
  226.9 1.9 broadcast_multiply_fusion.60
  293.2 1.8 broadcast_multiply_fusion.59
  294.9 1.9 broadcast_multiply_fusion.60
  361.2 1.8 broadcast_multiply_fusion.59
  363.0 1.9 broadcast_multiply_fusion.60
  429.2 1.8 broadcast_multiply_fusion.59
  431.0 1.9 broadcast_multiply_fusion.60
  497.3 1.8 broadcast_multiply_fusion.59
  499.1 1.9 broadcast_multiply_fusion.60
  565.3 1.8 broadcast_multiply_fusion.59
  567.1 1.9 broadcast_multiply_fusion.60
  633.4 1.8 broadcast_multiply_fusion.59
  635.2 1.9 broadcast_multiply_fusion.60
  676.8 5.6 collective-permute-done.4
  686.9 555.3 %collective-permute-start.10 = (f32[8,4]{0,1:T(4,128)S(1)}, f32[8,4]{0,1:T(4,128)S(1)}, u32[]{:S(2)}, u32[]{:S(2)}) collective-permute-start(f32[8,4]{0,1:T(4,128)S(1)} %copy.211), channel_id=1, source_target_pairs={{0,16},{1,17},{2,18},{3,19},{4,20},{5,21},{6,22},{7,23},{8,24},{9,... | collective-permute-start | bytes 392 | tf_op jit(solution)/shard_map/ppermute | solution.py:32
  1245.8 4.3 collective-permute-done.5
  1253.6 22.5 %scatter_custom_fusion = f32[3,96]{0,1:T(8,128)S(1)} fusion(s32[4096]{0:T(1024)} %bitcast.1043, f32[4096,3]{1,0:T(8,128)S(1)} %copy.208, f32[]{:T(128)} %constant.166.clone.1), kind=kCustom, calls=%fused_computation.701 | custom fusion | flops 12288 | bytes 1664 | tf_op jit(solution)/shard_map/scatter-add | solution.py:244
  1280.0 3.1 collective-permute-done.8
  (2775 shorter events, 531.9 us)
Async XLA Ops:
  0.6 10.6 copy-start
  4.2 33.8 %collective-permute-start.1 = (f32[1,1,4,8]{3,2,1,0:T(4,128)S(1)}, f32[1,1,4,8]{3,2,1,0:T(4,128)S(1)}, u32[]{:S(2)}, u32[]{:S(2)}) collective-permute-start(f32[1,1,4,8]{3,2,1,0:T(4,128)S(1)} %bitcast.1049), channel_id=1, source_target_pairs={{32,0},{64,32},{96,64},{128,96},{160,128},{192,160},{224,192},{0,2... | collective-permute-start | bytes 392 | tf_op jit(solution)/shard_map/ppermute | solution.py:24
  5.0 33.0 %collective-permute-start = (f32[1,1,4,8]{3,2,1,0:T(4,128)S(1)}, f32[1,1,4,8]{3,2,1,0:T(4,128)S(1)}, u32[]{:S(2)}, u32[]{:S(2)}) collective-permute-start(f32[1,1,4,8]{3,2,1,0:T(4,128)S(1)} %bitcast.1050), channel_id=1, source_target_pairs={{0,32},{32,64},{64,96},{96,128},{128,160},{160,192},{192,224},{224... | collective-permute-start | bytes 392 | tf_op jit(solution)/shard_map/ppermute | solution.py:22
  11.2 25.3 %copy-start.191 = (s32[16,256]{1,0:T(8,128)S(1)}, s32[16,256]{1,0:T(8,128)}, u32[]{:S(2)}) copy-start(s32[16,256]{1,0:T(8,128)} %param.25) | copy-start | bytes 49156
  38.0 22.1 %collective-permute-start.3 = (f32[3,1,4,8]{3,2,1,0:T(4,128)S(1)}, f32[3,1,4,8]{3,2,1,0:T(4,128)S(1)}, u32[]{:S(2)}, u32[]{:S(2)}) collective-permute-start(f32[3,1,4,8]{3,2,1,0:T(4,128)S(1)} %pad_maximum_fusion.3), channel_id=1, source_target_pairs={{1,0},{2,1},{3,2},{4,3},{5,4},{6,5},{7,6},{8,7},{9,8},{10,9},{11,1... | collective-permute-start | bytes 1160 | tf_op jit(solution)/shard_map/ppermute | solution.py:24
  60.1 6.7 collective-permute-start.2
  67.0 25.3 %copy-start.200 = (f32[3,64]{1,0:T(4,128)S(1)}, f32[3,64]{1,0:T(4,128)}, u32[]{:S(2)}) copy-start(f32[3,64]{1,0:T(4,128)} %param.21) | copy-start | bytes 2308
  113.8 22.0 %copy-start.139 = (f32[256]{0:T(256)}, f32[256]{0:T(256)S(1)}, u32[]{:S(2)}) copy-start(f32[256]{0:T(256)S(1)} %get-tuple-element.963) | copy-start | bytes 3076 | tf_op jit(solution)/shard_map/while
  125.4 14.5 %copy-start.31 = (f32[64,256]{1,0:T(8,128)}, f32[64,256]{1,0:T(8,128)S(1)}, u32[]{:S(2)}) copy-start(f32[64,256]{1,0:T(8,128)S(1)} %broadcast_in_dim.367) | copy-start | bytes 196612 | tf_op jit(solution)/shard_map/while
  181.9 22.0 %copy-start.139 = (f32[256]{0:T(256)}, f32[256]{0:T(256)S(1)}, u32[]{:S(2)}) copy-start(f32[256]{0:T(256)S(1)} %get-tuple-element.963) | copy-start | bytes 3076 | tf_op jit(solution)/shard_map/while
  193.4 14.5 %copy-start.31 = (f32[64,256]{1,0:T(8,128)}, f32[64,256]{1,0:T(8,128)S(1)}, u32[]{:S(2)}) copy-start(f32[64,256]{1,0:T(8,128)S(1)} %broadcast_in_dim.367) | copy-start | bytes 196612 | tf_op jit(solution)/shard_map/while
  249.9 22.0 %copy-start.139 = (f32[256]{0:T(256)}, f32[256]{0:T(256)S(1)}, u32[]{:S(2)}) copy-start(f32[256]{0:T(256)S(1)} %get-tuple-element.963) | copy-start | bytes 3076 | tf_op jit(solution)/shard_map/while
  259.3 10.3 copy-start.49
  261.5 14.5 %copy-start.31 = (f32[64,256]{1,0:T(8,128)}, f32[64,256]{1,0:T(8,128)S(1)}, u32[]{:S(2)}) copy-start(f32[64,256]{1,0:T(8,128)S(1)} %broadcast_in_dim.367) | copy-start | bytes 196612 | tf_op jit(solution)/shard_map/while
  317.9 22.0 %copy-start.139 = (f32[256]{0:T(256)}, f32[256]{0:T(256)S(1)}, u32[]{:S(2)}) copy-start(f32[256]{0:T(256)S(1)} %get-tuple-element.963) | copy-start | bytes 3076 | tf_op jit(solution)/shard_map/while
  329.5 14.5 %copy-start.31 = (f32[64,256]{1,0:T(8,128)}, f32[64,256]{1,0:T(8,128)S(1)}, u32[]{:S(2)}) copy-start(f32[64,256]{1,0:T(8,128)S(1)} %broadcast_in_dim.367) | copy-start | bytes 196612 | tf_op jit(solution)/shard_map/while
  386.0 22.0 %copy-start.139 = (f32[256]{0:T(256)}, f32[256]{0:T(256)S(1)}, u32[]{:S(2)}) copy-start(f32[256]{0:T(256)S(1)} %get-tuple-element.963) | copy-start | bytes 3076 | tf_op jit(solution)/shard_map/while
  397.5 14.5 %copy-start.31 = (f32[64,256]{1,0:T(8,128)}, f32[64,256]{1,0:T(8,128)S(1)}, u32[]{:S(2)}) copy-start(f32[64,256]{1,0:T(8,128)S(1)} %broadcast_in_dim.367) | copy-start | bytes 196612 | tf_op jit(solution)/shard_map/while
  454.0 22.0 %copy-start.139 = (f32[256]{0:T(256)}, f32[256]{0:T(256)S(1)}, u32[]{:S(2)}) copy-start(f32[256]{0:T(256)S(1)} %get-tuple-element.963) | copy-start | bytes 3076 | tf_op jit(solution)/shard_map/while
  465.6 14.5 %copy-start.31 = (f32[64,256]{1,0:T(8,128)}, f32[64,256]{1,0:T(8,128)S(1)}, u32[]{:S(2)}) copy-start(f32[64,256]{1,0:T(8,128)S(1)} %broadcast_in_dim.367) | copy-start | bytes 196612 | tf_op jit(solution)/shard_map/while
  522.1 22.0 %copy-start.139 = (f32[256]{0:T(256)}, f32[256]{0:T(256)S(1)}, u32[]{:S(2)}) copy-start(f32[256]{0:T(256)S(1)} %get-tuple-element.963) | copy-start | bytes 3076 | tf_op jit(solution)/shard_map/while
  533.6 14.5 %copy-start.31 = (f32[64,256]{1,0:T(8,128)}, f32[64,256]{1,0:T(8,128)S(1)}, u32[]{:S(2)}) copy-start(f32[64,256]{1,0:T(8,128)S(1)} %broadcast_in_dim.367) | copy-start | bytes 196612 | tf_op jit(solution)/shard_map/while
  590.1 22.0 %copy-start.139 = (f32[256]{0:T(256)}, f32[256]{0:T(256)S(1)}, u32[]{:S(2)}) copy-start(f32[256]{0:T(256)S(1)} %get-tuple-element.963) | copy-start | bytes 3076 | tf_op jit(solution)/shard_map/while
  601.7 14.5 %copy-start.31 = (f32[64,256]{1,0:T(8,128)}, f32[64,256]{1,0:T(8,128)S(1)}, u32[]{:S(2)}) copy-start(f32[64,256]{1,0:T(8,128)S(1)} %broadcast_in_dim.367) | copy-start | bytes 196612 | tf_op jit(solution)/shard_map/while
  674.0 8.4 collective-permute-start.4
  686.9 556.8 %collective-permute-start.10 = (f32[8,4]{0,1:T(4,128)S(1)}, f32[8,4]{0,1:T(4,128)S(1)}, u32[]{:S(2)}, u32[]{:S(2)}) collective-permute-start(f32[8,4]{0,1:T(4,128)S(1)} %copy.211), channel_id=1, source_target_pairs={{0,16},{1,17},{2,18},{3,19},{4,20},{5,21},{6,22},{7,23},{8,24},{9,... | collective-permute-start | bytes 392 | tf_op jit(solution)/shard_map/ppermute | solution.py:32
  1242.1 8.0 collective-permute-start.5
  1252.9 30.4 %copy-start.202 = (s32[8]{0:T(128)S(1)}, s32[8]{0:T(128)}, u32[]{:S(2)}) copy-start(s32[8]{0:T(128)} %copy-done.201) | copy-start | bytes 100
  1276.4 2.3 collective-permute-start.9
  1276.4 3.6 collective-permute-start.6
  1276.5 6.7 collective-permute-start.8
  1276.9 6.2 collective-permute-start.7
  (749 other events, 1906.6 us)
where the time goes:
time: 1300 us; the launch traced here: 1280 us
  starting transfers between devices  569 us (44%)
  local copies, waits for them, and re-layouts  273 us (21%)
  matrix products  207 us (16%)
  other arithmetic  180 us (14%)
  loops' own time  30.9 us (2%)
  waiting for transfers between devices  22.6 us (2%)
    ppermute x3, starting transfers between devices, partner(): lax.ppermute(shard, axis, [(i, i ^ 1 << bit) for i in range(lax.axis_size...  555 us
    dot_general x184, matrix products, matmul(): jnp.dot(left, right, precision=highest, preferred_element_type=jnp.float32)  146 us
    broadcast_in_dim x96, local copies, waits for them, and re-layouts, interaction(): gamma = jnp.broadcast_to(gamma, spread.shape).reshape(9, channels, pairs)  53.6 us
    another operation x2, loops' own time, run_blocks(): return lax.fori_loop(0, count, step, start)  30.9 us
    while x1528, local copies, waits for them, and re-layouts  29.1 us
    reshape x32, local copies, waits for them, and re-layouts, interaction(): gamma = jnp.broadcast_to(gamma, spread.shape).reshape(9, channels, pairs)  27.3 us
  transfers between devices with their start and end apart: 11, of which 6 were waited for; matrix products, arithmetic and copies ran while one was open for 4% of the time, Pallas kernels for 0%

commit v1 on v0

v1 whole, which is shorter than its diff:
```python
import functools
import math

import jax
import jax.numpy as jnp
from jax import lax
from jax.experimental import pallas as pl
from jax.experimental.pallas import tpu as pltpu
from jax.sharding import PartitionSpec as P

f32 = jnp.float32
bf16 = jnp.bfloat16
highest = lax.Precision.HIGHEST
SEG = 256
SLOTS = 8
LANES = 128
CH = 64
ROOT3 = math.sqrt(3.0)
ROOT5 = math.sqrt(5.0)
ROOT15 = math.sqrt(15.0)
HALF = math.sqrt(0.5)
ORDER = (0, 1, 1, 1, 2, 2, 2, 2, 2)
Y_V, Y_W0, Y_Z2, Y_Q = 0, 64, 128, 384
Q_W1, Q_GATE, Q_Z3, Q_OUT = 0, 64, 128, 384
D_W1, D_GATE, D_Z3, D_OUT, D_Z2, D_V, D_W0 = 0, 192, 384, 1152, 1536, 2304, 2496
D_ALL = 2688


def dot(left, right):
    return lax.dot_general(left, right, (((1,), (0,)), ((), ())), preferred_element_type=f32)


def dot_nt(left, right):
    return lax.dot_general(left, right, (((1,), (1,)), ((), ())), preferred_element_type=f32)


def split(value):
    high = value.astype(bf16)
    return high, (value - high.astype(f32)).astype(bf16)


def put3(ref, base, count, row, lanes, value):
    high, low = split(value)
    rows = value.shape[0]
    ref[pl.ds(base + row, rows), lanes] = high
    ref[pl.ds(base + count + row, rows), lanes] = high
    ref[pl.ds(base + 2 * count + row, rows), lanes] = low


def put2(high_ref, low_ref, row, lanes, value):
    high, low = split(value)
    rows = value.shape[0]
    high_ref[pl.ds(row, rows), lanes] = high
    low_ref[pl.ds(row, rows), lanes] = low


def prepare_kernel(
    emb2, v0, env, lat1, lat2, gate, mix, out1,
    ca, c0, lb0, lb1, c1, mx, cat, c0t, lb0t, lb1t, c1t, mxt, full, tall,
):
    def mul(left, right):
        return jnp.dot(left, right, precision=highest, preferred_element_type=f32)

    def triple(value):
        high, low = split(value)
        return jnp.concatenate([high, low, high], axis=1)

    def triple_t(target, column, value):
        high = value.astype(bf16).astype(f32)
        low = (value - high).astype(bf16).astype(f32)
        rows = value.shape[0]
        tall[pl.ds(column, rows), :] = high
        tall[pl.ds(column + rows, rows), :] = low
        tall[pl.ds(column + 2 * rows, rows), :] = high

    def turn(target, rows):
        for at in range(0, rows, LANES):
            target[:, at : at + LANES] = jnp.transpose(tall[at : at + LANES, :]).astype(bf16)

    late = jnp.concatenate(
        [env[1] * (0.125 * HALF), gate[0] * HALF, lat1[1][:, :256] * HALF, out1[...] * (HALF * HALF)],
        axis=0,
    )
    early = jnp.concatenate([v0[...], env[0] * 0.125, lat1[0][:, :256]], axis=0)
    full[0:384] = mul(early, emb2[...])
    full[384:896] = mul(late, emb2[...])
    ca[...] = triple(full[...])
    for column, start, rows in (
        (D_W1, 384, 64), (D_GATE, 448, 64), (D_Z3, 512, 256), (D_OUT, 768, 128),
        (D_Z2, 128, 256), (D_V, 0, 64), (D_W0, 64, 64),
    ):
        triple_t(cat, column, full[start : start + rows])
    turn(cat, D_ALL)
    full[0:512] = mul(late, lat2[0])
    c0[...] = triple(full[0:512])
    for column, start, rows in ((D_W1, 0, 64), (D_GATE, 64, 64), (D_Z3, 128, 256), (D_OUT, 384, 128)):
        triple_t(c0t, column, full[start : start + rows])
    turn(c0t, 1536)
    full[0:128] = mul(out1[...] * HALF, lat2[1])
    c1[...] = triple(full[0:128])
    triple_t(c1t, 0, full[0:128])
    turn(c1t, 384)
    for layer, ahead, back in ((0, lb0, lb0t), (1, lb1, lb1t)):
        part = lat1[layer][:, 256:448]
        ahead[...] = triple(part)
        back[...] = triple(jnp.transpose(part))
    for order in range(3):
        mx[order] = triple(mix[0, order])
        mxt[order] = triple(jnp.transpose(mix[0, order]))


def prepare(emb2, v0, env, lat1, lat2, gate, mix, out1):
    shapes = [
        (896, 768), (512, 768), (256, 576), (256, 576), (128, 768), (3, 64, 192),
        (256, D_ALL), (256, 1536), (192, 768), (192, 768), (256, 384), (3, 64, 192),
    ]
    return pl.pallas_call(
        prepare_kernel,
        out_shape=[jax.ShapeDtypeStruct(s, bf16) for s in shapes],
        in_specs=[pl.BlockSpec(memory_space=pltpu.VMEM)] * 8,
        out_specs=[pl.BlockSpec(memory_space=pltpu.VMEM)] * len(shapes),
        scratch_shapes=[pltpu.VMEM((896, 256), f32), pltpu.VMEM((D_ALL, 256), f32)],
        compiler_params=pltpu.CompilerParams(vmem_limit_bytes=40 * 2**20),
        name="prepare",
    )(emb2, v0, env, lat1, lat2, gate, mix, out1)


def scratch_list(width):
    w, s = width, width // SEG
    return dict(
        oh=((256, w), bf16), sb=((256, w), bf16), sf=((SLOTS, w), f32), hb=((256, w), bf16),
        x1=((64, w), bf16), a=((768, w), bf16), s0=((576, w), bf16), b=((768, w), bf16),
        s1=((576, w), bf16), c=((768, w), bf16), dy=((D_ALL, w), bf16),
        u=((1728, w), bf16), dt=((1728, w), bf16), dg=((576, 2 * w), bf16),
        wh=((320, w), bf16), wl=((320, w), bf16),
        y=((896, w), f32), q=((512, w), f32),
        sa=((256, w), f32), da=((256, w), f32), sbb=((256, w), f32), dbb=((256, w), f32),
        sc=((256, w), f32), dc=((256, w), f32),
        a0=((192, w), f32), g0=((576, w), f32), g1=((576, w), f32), bm=((576, w), f32),
        t=((576, w), f32), du=((576, w), f32), vg=((64, w), f32), dv=((64, w), f32),
        gm=((2 * s, 64, LANES), f32), gd=((2 * s, 64, LANES), f32),
    )


NAMES = tuple(scratch_list(512))


class Stream:
    def __init__(self, refs, width):
        for name, ref in zip(NAMES, refs):
            setattr(self, name, ref)
        self.width = width
        self.segs = [slice(i * SEG, (i + 1) * SEG) for i in range(width // SEG)]
        self.all = slice(0, width)


def order_mask(order):
    lane = lax.broadcasted_iota(jnp.int32, (64, LANES), 1)
    low, high = ((0, 8), (8, 32), (32, 72))[order]
    return (lane >= low) & (lane < high)


def sublane_sum(value):
    return jnp.sum(value, axis=0, keepdims=True)


def fold(value):
    rows, lanes = value.shape
    return jnp.sum(value.reshape(rows // 8, 8, lanes), axis=0)


def pack(work, counts, tab, nbr, lanes, st, state):
    item, center = state
    owner = work[item, 0]
    last = work[item, 2]
    lane = lax.broadcasted_iota(jnp.int32, (1, SEG), 1)
    slot_row = lax.broadcasted_iota(jnp.int32, (SLOTS, SEG), 0)
    slot_lane = lax.broadcasted_iota(jnp.int32, (SLOTS, SEG), 1)
    inside = jnp.zeros((SLOTS, SEG), jnp.bool_)
    names = jnp.full((1, SEG), -1, jnp.int32)
    mine = jnp.full((1, SEG), -1, jnp.int32)
    filled = jnp.int32(0)
    going = jnp.bool_(True)
    taken = jnp.int32(0)
    for j in range(SLOTS):
        at = jnp.minimum(center + j, 63)
        count = counts[owner, at]
        going = going & (center + j < last) & (filled + count <= SEG)
        count = jnp.where(going, count, 0)
        row = nbr[pl.ds(owner * 64 + at, 1), :]
        row = jnp.concatenate([row, row], axis=1)
        row = pltpu.roll(row, filled, axis=1)
        here = (lane >= filled) & (lane < filled + count)
        names = jnp.where(here, row, names)
        mine = jnp.where(here, at, mine)
        inside = inside | (
            (slot_row == j) & (slot_lane >= filled) & (slot_lane < filled + count)
        )
        filled = filled + count
        taken = taken + going.astype(jnp.int32)
    seats = inside.astype(f32)
    st.sf[:, lanes] = seats
    both = jnp.concatenate([seats, jnp.zeros_like(seats)], axis=0).astype(bf16)
    st.sb[0:16, lanes] = both
    st.sb[128:144, lanes] = both
    for row in range(0, LANES, 32):
        atom = lax.broadcasted_iota(jnp.int32, (32, SEG), 0) + row
        st.oh[row : row + 32, lanes] = (atom == names).astype(f32).astype(bf16)
        st.oh[LANES + row : LANES + row + 32, lanes] = (atom == mine).astype(f32).astype(bf16)
    gathered = dot(tab[owner], st.oh[:, lanes])
    center = center + taken
    ended = center >= last
    item = jnp.where(ended, item + 1, item)
    center = jnp.where(ended, work[item, 1], center)
    return (item, center), owner, gathered


def spread(seg_gamma, seats):
    parts = [
        seg_gamma if m == 0 else pltpu.roll(seg_gamma, LANES - 8 * m, axis=1) for m in range(9)
    ]
    high, low = split(jnp.concatenate(parts, axis=0))
    return dot(jnp.concatenate([high, low], axis=1), seats)


def gather_gamma(parts):
    total = parts[0:64]
    for m in range(1, 9):
        total = total + pltpu.roll(parts[64 * m : 64 * m + 64], 8 * m, axis=1)
    return total


def with_harmonics(value, hb):
    high, low = split(value)
    return dot(jnp.concatenate([high, high], axis=1), hb) + dot(low, hb[0:LANES])


def over_harmonics(high, low, hb):
    first = dot_nt(high, hb)
    return first[:, :LANES] + first[:, LANES:] + dot_nt(low, hb[0:LANES])


def gate_curve(value):
    sig = 0.5 * jnp.tanh(0.5 * value) + 0.5
    act = value * sig
    return act, sig + act * (1.0 - sig)


def activate(st, product, base_ref, base_row, act_ref, slope_ref, target, env):
    for lanes in st.segs:
        scale = env[:, lanes]
        for row in range(0, 256, 32):
            value = product[row : row + 32, lanes]
            if base_ref is not None:
                value = value + base_ref[base_row + row : base_row + row + 32, lanes]
            act, slope = gate_curve(value)
            act_ref[row : row + 32, lanes] = act
            slope_ref[row : row + 32, lanes] = slope * scale
            put3(target, 0, 256, row, lanes, act * scale)


def deactivate(st, product, act_ref, slope_ref, target, base):
    sums = []
    for lanes in st.segs:
        total = jnp.zeros((8, SEG), f32)
        for row in range(0, 256, 32):
            value = product[row : row + 32, lanes]
            total = total + fold(value * act_ref[row : row + 32, lanes])
            put3(target, base, 256, row, lanes, value * slope_ref[row : row + 32, lanes])
        sums.append(sublane_sum(total))
    return jnp.concatenate(sums, axis=1)


def tile(st, w, work, counts, tab, nbr, out, state):
    ca, c0, lb0, lb1, c1, mx, cat, c0t, lb0t, lb1t, c1t, mxt, w1, e1t, w2 = w
    owners, gathered = [], []
    for lanes in st.segs:
        state, owner, got = pack(work, counts, tab, nbr, lanes, st, state)
        owners.append(owner)
        gathered.append(got)
    got = jnp.concatenate(gathered, axis=1) if len(gathered) > 1 else gathered[0]
    off = got[0:8] + got[8:16] + got[16:24]
    ox, oy, oz = off[0:1], off[1:2], off[2:3]
    st.x1[0:16, :] = got[24:40].astype(bf16)
    st.x1[16:32, :] = got[24:40].astype(bf16)
    dist_sq = ox * ox + oy * oy + oz * oz + 0.25
    dist = jnp.sqrt(dist_sq)
    inv = 1.0 / dist
    ux, uy, uz = ox * inv, oy * inv, oz * inv
    harm = [
        None, ROOT3 * ux, ROOT3 * uy, ROOT3 * uz, ROOT15 * ux * uy, ROOT15 * uy * uz,
        0.5 * ROOT5 * (2.0 * uz * uz - ux * ux - uy * uy), ROOT15 * ux * uz,
        0.5 * ROOT15 * (ux * ux - uy * uy),
    ]
    ratio = dist_sq * 0.0625
    env = 1.0 / (1.0 + ratio * ratio)
    angle = dist * (math.pi / 8.0)
    sin1, cos1 = jnp.sin(angle), jnp.cos(angle)
    sines, cosines = [sin1], [cos1]
    for _ in range(7):
        s, c = sines[-1], cosines[-1]
        sines.append(s * cos1 + c * sin1)
        cosines.append(c * cos1 - s * sin1)
    sines, cosines = jnp.concatenate(sines, axis=0), jnp.concatenate(cosines, axis=0)
    level = 0.5 * inv * env
    high = (sines * level).astype(bf16).astype(f32)
    pair = jnp.concatenate([high, sines * level - high], axis=0).astype(bf16)
    st.x1[32:48, :] = pair
    st.x1[48:64, :] = pair
    for lanes in st.segs:
        seats = st.sf[:, lanes]
        blocks = [seats] + [harm[m][:, lanes] * seats for m in range(1, 9)] + [jnp.zeros_like(seats)]
        for k in range(0, 10, 2):
            block = jnp.concatenate(blocks[k : k + 2], axis=0)
            h, l = split(block)
            st.hb[8 * k : 8 * k + 16, lanes] = h
            st.hb[LANES + 8 * k : LANES + 8 * k + 16, lanes] = l
    activate(st, dot(w1[...], st.x1[...]), None, 0, st.sa, st.da, st.a, env)
    st.y[...] = dot(ca[...], st.a[...])
    for i, lanes in enumerate(st.segs):
        put2(st.wh, st.wl, 64, lanes, st.y[Y_W0 : Y_W0 + 64, lanes])
        hb = st.hb[:, lanes]
        gamma = over_harmonics(st.wh[64:128, lanes], st.wl[64:128, lanes], hb)
        st.gm[i] = gamma
        masked = jnp.concatenate([jnp.where(order_mask(l), gamma, 0.0) for l in range(3)], axis=0)
        scale = with_harmonics(masked, hb)
        st.a0[:, lanes] = scale
        for row in range(0, 192, 32):
            value = st.y[Y_V + row % 64 : Y_V + row % 64 + 32, lanes]
            put3(st.s0, 0, 192, row, lanes, value * scale[row : row + 32])
    activate(st, dot(lb0[...], st.s0[...]), st.y, Y_Z2, st.sbb, st.dbb, st.b, env)
    st.q[...] = dot(c0[...], st.b[...]) + st.y[Y_Q : Y_Q + 512, :]
    for i, lanes in enumerate(st.segs):
        st.g0[:, lanes] = spread(st.gm[i], st.sb[:, lanes])
        put2(st.wh, st.wl, 0, lanes, st.q[Q_W1 : Q_W1 + 64, lanes])
        hb = st.hb[:, lanes]
        gamma = over_harmonics(st.wh[0:64, lanes], st.wl[0:64, lanes], hb)
        st.gm[len(st.segs) + i] = gamma
        st.g1[:, lanes] = spread(gamma, st.sb[:, lanes])
    for lanes in st.segs:
        h = [None] + [harm[m][:, lanes] for m in range(1, 9)]
        for row in range(0, 64, 16):
            vg = st.y[Y_V + row : Y_V + row + 16, lanes] * st.q[Q_GATE + row : Q_GATE + row + 16, lanes]
            st.vg[row : row + 16, lanes] = vg
            g = [st.g0[64 * m + row : 64 * m + row + 16, lanes] for m in range(9)]
            mixed = [g[0]] + [g[m] + g[0] * h[m] for m in range(1, 9)]
            mixed[1] = mixed[1] + (h[2] * g[3] - h[3] * g[2])
            mixed[2] = mixed[2] + (h[3] * g[1] - h[1] * g[3])
            mixed[3] = mixed[3] + (h[1] * g[2] - h[2] * g[1])
            for m in range(9):
                st.bm[64 * m + row : 64 * m + row + 16, lanes] = mixed[m]
                put3(st.u, 192 * m, 64, row, lanes, vg * mixed[m])
    for m in range(9):
        st.t[64 * m : 64 * m + 64, :] = dot(mx[ORDER[m]], st.u[192 * m : 192 * m + 192, :])
    for lanes in st.segs:
        for row in range(0, 64, 16):
            total = [None, None, None]
            for m in range(9):
                at = slice(64 * m + row, 64 * m + row + 16)
                term = st.t[at, lanes] * st.g1[at, lanes]
                o = ORDER[m]
                total[o] = term if total[o] is None else total[o] + term
            for o in range(3):
                put3(st.s1, 0, 192, 64 * o + row, lanes, total[o])
    activate(st, dot(lb1[...], st.s1[...]), st.q, Q_Z3, st.sc, st.dc, st.c, env)
    final = dot(c1[...], st.c[...])
    valid = sublane_sum(st.sf[...])
    reads = []
    for lanes in st.segs:
        total = jnp.zeros((8, SEG), f32)
        scale = env[:, lanes] * valid[:, lanes]
        for row in range(0, 128, 32):
            value = final[row : row + 32, lanes] + st.q[Q_OUT + row : Q_OUT + row + 32, lanes]
            act, slope = gate_curve(value)
            weight = w2[row : row + 32, :]
            weight = jnp.concatenate([weight, weight], axis=1)
            total = total + fold(act * weight)
            put3(st.dy, D_OUT, 128, row, lanes, slope * weight * scale)
        reads.append(sublane_sum(total))
    read = jnp.concatenate(reads, axis=1) * valid
    energy = read * env
    d_env = deactivate(st, dot(c1t[...], st.dy[D_OUT : D_OUT + 384, :]), st.sc, st.dc, st.dy, D_Z3)
    d_scal = dot(lb1t[...], st.dy[D_Z3 : D_Z3 + 768, :])
    for i, lanes in enumerate(st.segs):
        for row in range(0, 64, 16):
            for m in range(9):
                at = slice(64 * m + row, 64 * m + row + 16)
                part = d_scal[64 * ORDER[m] + row : 64 * ORDER[m] + row + 16, lanes]
                put3(st.dt, 192 * m, 64, row, lanes, st.g1[at, lanes] * part)
                high, low = split(st.t[at, lanes] * part)
                st.dg[at, 2 * SEG * i : 2 * SEG * i + SEG] = high
                st.dg[at, 2 * SEG * i + SEG : 2 * SEG * i + 2 * SEG] = low
    for i, lanes in enumerate(st.segs):
        seats = st.sb[0:LANES, lanes]
        seats = jnp.concatenate([seats, seats], axis=1)
        d_gamma = gather_gamma(dot_nt(st.dg[:, 2 * SEG * i : 2 * SEG * i + 2 * SEG], seats))
        st.gd[len(st.segs) + i] = d_gamma
        d_weight = with_harmonics(d_gamma, st.hb[:, lanes])
        put3(st.dy, D_W1, 64, 0, lanes, d_weight)
    for m in range(9):
        st.du[64 * m : 64 * m + 64, :] = dot(mxt[ORDER[m]], st.dt[192 * m : 192 * m + 192, :])
    d_harm = []
    for i, lanes in enumerate(st.segs):
        h = [None] + [harm[m][:, lanes] for m in range(1, 9)]
        sums = [jnp.zeros((8, SEG), f32) for _ in range(8)]
        for row in range(0, 64, 16):
            rows = slice(row, row + 16)
            vg = st.vg[rows, lanes]
            d_vg = jnp.zeros((16, SEG), f32)
            d = []
            for m in range(9):
                at = slice(64 * m + row, 64 * m + row + 16)
                grad = st.du[at, lanes]
                d_vg = d_vg + grad * st.bm[at, lanes]
                d.append(grad * vg)
            value = st.y[Y_V + row : Y_V + row + 16, lanes]
            gate = st.q[Q_GATE + row : Q_GATE + row + 16, lanes]
            put3(st.dy, D_GATE, 64, row, lanes, value * d_vg)
            st.dv[rows, lanes] = gate * d_vg
            g = [st.g0[64 * m + row : 64 * m + row + 16, lanes] for m in range(4)]
            terms = [g[0] * d[m] for m in range(1, 9)]
            terms[0] = terms[0] + (g[2] * d[3] - g[3] * d[2])
            terms[1] = terms[1] + (g[3] * d[1] - g[1] * d[3])
            terms[2] = terms[2] + (g[1] * d[2] - g[2] * d[1])
            sums = [a + fold(b) for a, b in zip(sums, terms)]
            first = d[0]
            for m in range(1, 9):
                first = first + h[m] * d[m]
            back = [first] + d[1:]
            back[1] = back[1] + (h[3] * d[2] - h[2] * d[3])
            back[2] = back[2] + (h[1] * d[3] - h[3] * d[1])
            back[3] = back[3] + (h[2] * d[1] - h[1] * d[2])
            for m in range(9):
                at = slice(64 * m + row, 64 * m + row + 16)
                high, low = split(back[m])
                st.dg[at, 2 * SEG * i : 2 * SEG * i + SEG] = high
                st.dg[at, 2 * SEG * i + SEG : 2 * SEG * i + 2 * SEG] = low
        d_harm.append([sublane_sum(x) for x in sums])
    d_env = d_env + deactivate(st, dot(c0t[...], st.dy[0:1536, :]), st.sbb, st.dbb, st.dy, D_Z2)
    d_scal = dot(lb0t[...], st.dy[D_Z2 : D_Z2 + 768, :])
    for i, lanes in enumerate(st.segs):
        for row in range(0, 64, 32):
            rows = slice(row, row + 32)
            value = st.y[Y_V + row : Y_V + row + 32, lanes]
            d_value = st.dv[rows, lanes]
            for o in range(3):
                at = slice(64 * o + row, 64 * o + row + 32)
                part = d_scal[at, lanes]
                d_value = d_value + part * st.a0[at, lanes]
                put2(st.wh, st.wl, 128 + 64 * o + row, lanes, value * part)
            put3(st.dy, D_V, 64, row, lanes, d_value)
        hb = st.hb[:, lanes]
        seats = st.sb[0:LANES, lanes]
        seats = jnp.concatenate([seats, seats], axis=1)
        d_gamma = gather_gamma(dot_nt(st.dg[:, 2 * SEG * i : 2 * SEG * i + 2 * SEG], seats))
        d_scale = over_harmonics(st.wh[128:320, lanes], st.wl[128:320, lanes], hb)
        for o in range(3):
            d_gamma = d_gamma + jnp.where(order_mask(o), d_scale[64 * o : 64 * o + 64], 0.0)
        put3(st.dy, D_W0, 64, 0, lanes, with_harmonics(d_gamma, hb))
        gamma = st.gm[i]
        left = [st.gd[len(st.segs) + i], d_gamma]
        left = left + [jnp.where(order_mask(l), gamma, 0.0) for l in range(3)]
        left = jnp.concatenate([jnp.transpose(x) for x in (
            jnp.concatenate(left[0:2], axis=0), jnp.concatenate(left[2:4], axis=0),
            jnp.concatenate([left[4], jnp.zeros((64, LANES), f32)], axis=0),
        )], axis=1)
        high, low = split(left[0:80])
        high, low = high[:, 0:320], low[:, 0:320]
        d_seated = (
            dot(high, st.wh[:, lanes]) + dot(low, st.wh[:, lanes]) + dot(high, st.wl[:, lanes])
        )
        seats = st.sf[:, lanes]
        for m in range(1, 9):
            d_harm[i][m - 1] = d_harm[i][m - 1] + sublane_sum(d_seated[8 * m : 8 * m + 8] * seats)
    d_env = d_env + deactivate(st, dot(cat[...], st.dy[...]), st.sa, st.da, st.a, 0)
    d_basis = dot(e1t[...], st.a[...])[0:8]
    d_env = d_env + read
    dh = [None] + [jnp.concatenate([x[m] for x in d_harm], axis=1) for m in range(8)]
    dux = ROOT3 * dh[1] + ROOT15 * (uy * dh[4] + uz * dh[7] + ux * dh[8]) - ROOT5 * ux * dh[6]
    duy = ROOT3 * dh[2] + ROOT15 * (ux * dh[4] + uz * dh[5] - uy * dh[8]) - ROOT5 * uy * dh[6]
    duz = ROOT3 * dh[3] + ROOT15 * (uy * dh[5] + ux * dh[7]) + 2.0 * ROOT5 * uz * dh[6]
    order = (lax.broadcasted_iota(jnp.int32, (8, st.width), 0) + 1).astype(f32)
    sine_part = sublane_sum(sines * d_basis)
    cos_part = sublane_sum(order * cosines * d_basis)
    d_env = d_env + 0.5 * inv * sine_part
    d_inv = 0.5 * env * sine_part + ox * dux + oy * duy + oz * duz
    d_dist = (math.pi / 8.0) * level * cos_part
    d_sq = -0.125 * ratio * env * env * d_env + 0.5 * inv * d_dist - 0.5 * inv * inv * inv * d_inv
    d_sq = 2.0 * d_sq
    grad = [inv * dux + d_sq * ox, inv * duy + d_sq * oy, inv * duz + d_sq * oz]
    rows = jnp.concatenate(grad + [energy, jnp.zeros((4, st.width), f32)], axis=0)
    row_id = lax.broadcasted_iota(jnp.int32, (8, LANES), 0)
    for i, lanes in enumerate(st.segs):
        high = rows[:, lanes].astype(bf16).astype(f32)
        low = rows[:, lanes] - high
        sent = dot_nt(jnp.concatenate([high, low], axis=0).astype(bf16), st.oh[:, lanes])
        sent = sent[0:8] + sent[8:16]
        other, own = sent[:, :LANES], sent[:, LANES:]
        out[owners[i]] = out[owners[i]] + jnp.where(row_id < 3, own - other, own)
    return state


def force_kernel(width, owners, work, counts, ext, nbr, *rest):
    weights, out = rest[:15], rest[15]
    tab, scratch = rest[16], rest[17:]
    st = Stream(scratch, width)
    out[...] = jnp.zeros_like(out)
    st.sb[...] = jnp.zeros_like(st.sb)
    st.hb[...] = jnp.zeros_like(st.hb)
    kind = lax.broadcasted_iota(jnp.int32, (8, LANES), 0).astype(f32)
    row = lax.broadcasted_iota(jnp.int32, (8, LANES), 0)
    for owner in range(owners):
        value = ext[owner]
        place = jnp.where(row < 3, value, 0.0)
        high = place.astype(bf16).astype(f32)
        rest_of = place - high
        mid = rest_of.astype(bf16).astype(f32)
        low = (rest_of - mid).astype(bf16).astype(f32)
        named = (kind == value[3:4]).astype(f32)
        none = jnp.zeros_like(named)
        first = jnp.concatenate([high, mid, low, none, named, none], axis=0)
        second = jnp.concatenate([-high, -mid, -low, named, none, none], axis=0)
        tab[owner] = jnp.concatenate([first, second], axis=1).astype(bf16)
    total = work[4, 0]

    def step(state):
        return tile(st, weights, work, counts, tab, nbr, out, state)

    lax.while_loop(lambda s: s[0] < total, step, (jnp.int32(0), work[0, 1]))


def run_forces(work, counts, ext, nbr, weights, width=512):
    owners = ext.shape[0]
    scratch = scratch_list(width)
    vmem = pl.BlockSpec(memory_space=pltpu.VMEM)
    smem = pl.BlockSpec(memory_space=pltpu.SMEM)
    return pl.pallas_call(
        functools.partial(force_kernel, width, owners),
        out_shape=jax.ShapeDtypeStruct((owners, 8, LANES), f32),
        in_specs=[smem, smem, vmem, vmem] + [vmem] * len(weights),
        out_specs=vmem,
        scratch_shapes=[pltpu.VMEM((owners, 48, 256), bf16)]
        + [pltpu.VMEM(shape, kind) for shape, kind in scratch.values()],
        compiler_params=pltpu.CompilerParams(vmem_limit_bytes=52 * 2**20),
        name="forces",
    )(work, counts, ext, nbr, *weights)


def all_weights(w_embed1, w_embed2, w_v0, w_env, w_lat1, w_lat2, w_gate, w_mix, w_out1, w_out2):
    prepared = prepare(w_embed2, w_v0, w_env, w_lat1, w_lat2, w_gate, w_mix, w_out1)
    high = lax.reduce_precision(w_embed1, 8, 7)
    low = w_embed1 - high
    kinds = w_embed1.shape[1] - 8
    kh, kl, bh, bl = high[:, :kinds], low[:, :kinds], high[:, kinds:], low[:, kinds:]
    first = jnp.concatenate([kh, kl, bh, bh, bl, bl], axis=1).astype(bf16)
    back = jnp.concatenate([bh.T, bl.T, bh.T], axis=1)
    back = jnp.pad(back, ((0, 8), (0, 0))).astype(bf16)
    wide = jnp.broadcast_to(w_out2[:, None], (w_out2.shape[0], LANES))
    return tuple(prepared) + (first, back, wide)


def beside(cells, axis, step):
    count = lax.axis_size(axis)
    return lax.ppermute(cells, axis, [(i, (i + step) % count) for i in range(count)])


def local(
    positions,
    species,
    ghost_index,
    bin_load,
    neighbour,
    pair_count,
    species_shift,
    w_embed1,
    w_embed2,
    w_v0,
    w_env,
    w_lat1,
    w_lat2,
    w_gate,
    w_mix,
    w_out1,
    w_out2,
):
    atoms = positions.shape[1]
    bins, pairs = neighbour.shape
    centers = pair_count.shape[1]
    ghosts = ghost_index.shape[0]
    load = bin_load[0]
    named = ghost_index[:, None] == jnp.arange(atoms)[None, :]
    whole = jnp.concatenate([positions, species.astype(f32)[None]], axis=0)
    shell = jnp.sum(jnp.where(named[None], whole[:, None, :], 0.0), axis=2)
    received = [beside(shell, "grp", 1), beside(shell, "grp", -1), beside(shell, "dom", 1), beside(shell, "dom", -1)]
    weights = all_weights(
        w_embed1, w_embed2, w_v0, w_env, w_lat1, w_lat2, w_gate, w_mix, w_out1, w_out2
    )
    ext = jnp.concatenate([whole] + received, axis=1)
    ext = jnp.pad(ext, ((0, 4), (0, LANES - ext.shape[1])))[None]
    names = jnp.pad(neighbour.reshape(bins * centers, pairs // centers), ((0, 0), (0, 64)))
    counts = pair_count.reshape(1, bins * centers)
    end = load * centers
    zero = jnp.int32(0)
    row = jnp.stack([zero, zero, end, zero])
    work = jnp.zeros((8, 4), jnp.int32).at[0].set(row).at[4, 0].set(1)
    result = run_forces(work, counts, ext, names, weights)[0]
    energies = result[3, :atoms]
    force = result[0:3, :atoms]
    ghost = result[0:3, atoms : atoms + 4 * ghosts].reshape(3, 4, ghosts)
    back = (
        beside(ghost[:, 0], "grp", -1)
        + beside(ghost[:, 1], "grp", 1)
        + beside(ghost[:, 2], "dom", -1)
        + beside(ghost[:, 3], "dom", 1)
    )
    forces = force + jnp.sum(jnp.where(named[None], back[:, :, None], 0.0), axis=1)
    live = jnp.arange(atoms) // centers < load
    kind_range = jnp.arange(species_shift.shape[0])
    shift = jnp.sum(
        jnp.where(species[:, None] == kind_range[None], species_shift[None, :], 0.0), axis=1
    )
    return (forces, energies + jnp.where(live, shift, 0.0))


def solution(mesh):
    spread_over = ("grp", "dom")
    in_specs = (
        P(None, spread_over),
        P(spread_over),
        P(spread_over),
        P(spread_over),
        P(spread_over, None),
        P(spread_over, None),
    ) + (P(),) * 11
    out_specs = (P(None, spread_over), P(spread_over))
    return jax.shard_map(local, mesh=mesh, in_specs=in_specs, out_specs=out_specs, check_vma=False)
```

time: 1300 us -> 113 us (0.09)
  the two profiles are of different devices: /device:TPU:6 before, /device:TPU:56 now
where the time goes in v1:
time: 113 us
  starting transfers between devices  63.6 us (56%)
  Pallas kernels  22.8 us (20%)
  local copies, waits for them, and re-layouts  15.4 us (14%)
  waiting for transfers between devices  5.18 us (5%)
  other arithmetic  4.16 us (4%)
  between operations  1.57 us (1%)
    ppermute x8, starting transfers between devices, beside(): lax.ppermute(cells, axis, [(i, (i + step) % count) for i in range(count)])  63.6 us
    pallas_call x1, Pallas kernels, run_forces(): pl.pallas_call(functools.partial(force_kernel, width, owners), out_shape=...  20.9 us
    unnamed x49, local copies, waits for them, and re-layouts  12.7 us
    ppermute x8, waiting for transfers between devices, beside(): lax.ppermute(cells, axis, [(i, (i + step) % count) for i in range(count)])  5.18 us
  transfers between devices with their start and end apart: 8, of which 2 were waited for; matrix products, arithmetic and copies ran while one was open for 4% of the time, Pallas kernels for 2%

profile of v1, /device:TPU:56, one launch (start us, length us, event | category | flops | bytes accessed | tf_op | source)
XLA Modules:
  0.0 112.7 jit_solution(6967055362747030535)
XLA Ops:
  0.7 0.8 convert_bitcast_fusion
  1.5 0.7 iota_compare_fusion.2
  2.2 0.7 pad_maximum_fusion
  3.0 1.5 %collective-permute-start = (f32[4,8]{1,0:T(4,128)S(1)}, f32[4,8]{1,0:T(4,128)S(1)}, u32[]{:S(2)}, u32[]{:S(2)}) collective-permute-start(f32[4,8]{1,0:T(4,128)S(1)} %select_reduce_fusion), channel_id=1, source_target_pairs={{0,32},{32,64},{64,96},{96,128},{128,160},{160,192},{192,224},{224... | collective-permute-start | bytes 392 | tf_op jit(solution)/shard_map/ppermute | solution.py:564
  4.5 2.6 %collective-permute-start.1 = (f32[4,8]{1,0:T(4,128)S(1)}, f32[4,8]{1,0:T(4,128)}, u32[]{:S(2)}, u32[]{:S(2)}) collective-permute-start(f32[4,8]{1,0:T(4,128)S(1)} %select_reduce_fusion), channel_id=1, source_target_pairs={{0,224},{32,0},{64,32},{96,64},{128,96},{160,128},{192,160},{224,1... | collective-permute-start | bytes 392 | tf_op jit(solution)/shard_map/ppermute | solution.py:564
  7.1 3.2 %collective-permute-start.3 = (f32[4,8]{1,0:T(4,128)S(1)}, f32[4,8]{1,0:T(4,128)}, u32[]{:S(2)}, u32[]{:S(2)}) collective-permute-start(f32[4,8]{1,0:T(4,128)S(1)} %select_reduce_fusion), channel_id=1, source_target_pairs={{0,31},{1,0},{2,1},{3,2},{4,3},{5,4},{6,5},{7,6},{8,7},{9,8},{10,9... | collective-permute-start | bytes 392 | tf_op jit(solution)/shard_map/ppermute | solution.py:564
  11.1 0.8 copy.25
  12.0 0.8 reshape.95
  12.8 1.5 %copy.26.lat1 = f32[2,256,448]{2,1,0:T(8,128)S(1)} copy(f32[2,256,448]{1,2,0:T(8,128)} %param.32) | data formatting | bytes 1835008 | tf_op args[11]
  14.5 0.6 select_reduce_fusion.2
  15.2 0.9 copy-done.9
  16.1 0.8 copy-done.14
  16.9 0.8 copy-done.15
  17.8 1.9 %prepare.1 = (bf16[896,768]{1,0:T(8,128)(2,1)S(1)}, bf16[512,768]{1,0:T(8,128)(2,1)S(1)}, bf16[256,576]{1,0:T(8,128)(2,1)S(1)}, bf16[256,576]{1,0:T(8,128)(2,1)S...) custom-call(f32[256,256]{1,0:T(8,128)S(1)} %copy-done.6, ...), custom_call_target="tpu_custom_call" | custom-call | tf_op jit(solution)/shard_map/prepare/pallas_call | solution.py:117
  19.7 1.1 copy-done
  20.8 1.1 copy-done.1
  21.9 0.9 copy-done.2
  22.7 0.9 copy-done.3
  23.6 0.7 copy-done.5
  24.4 0.6 copy-done.10
  25.0 0.6 copy-done.12
  25.7 0.8 concatenate.19
  26.5 0.7 broadcast_in_dim.83.rest_14_
  27.2 0.9 copy-done.11
  28.1 0.9 copy-done.13
  29.0 20.9 %forces.1 = f32[1,8,128]{2,1,0:T(8,128)S(1)} custom-call(s32[8,4]{1,0:T(8,128)S(1)} %scatter.9.work, s32[1,64]{1,0:T(1,128)S(1)} %reshape.94.counts, f32[1,8,128]{2,1,0:T(8,128)S(1)} %pad_bitcast_fusion.ext, s32[64,128]{1,0:T(8,128)S(1)} %pad.21.nbr, bf16[896,768]{1,0:T(8,128)(2,1)} %copy-done, bf16[512,768]{1,0:T(8,128)(2,1)} %copy-done.2, ...), custom_call_target="tpu_custom_call" | custom-call | tf_op jit(solution)/shard_map/forces/pallas_call | solution.py:537
  50.2 9.3 %collective-permute-start.6 = (f32[3,8]{1,0:T(4,128)S(1)}, f32[3,8]{1,0:T(4,128)S(1)}, u32[]{:S(2)}, u32[]{:S(2)}) collective-permute-start(f32[3,8]{1,0:T(4,128)S(1)} %bitcast.33), channel_id=1, source_target_pairs={{0,31},{1,0},{2,1},{3,2},{4,3},{5,4},{6,5},{7,6},{8,7},{9,8},{10,9... | collective-permute-start | bytes 296 | tf_op jit(solution)/shard_map/ppermute | solution.py:564
  59.5 46.8 %collective-permute-start.4 = (f32[3,8]{1,0:T(4,128)S(1)}, f32[3,8]{1,0:T(4,128)S(1)}, u32[]{:S(2)}, u32[]{:S(2)}) collective-permute-start(f32[3,8]{1,0:T(4,128)S(1)} %bitcast.34), channel_id=1, source_target_pairs={{0,224},{32,0},{64,32},{96,64},{128,96},{160,128},{192,160},{224,1... | collective-permute-start | bytes 296 | tf_op jit(solution)/shard_map/ppermute | solution.py:564
  106.3 0.5 fusion.5
  106.8 0.8 collective-permute-done.4
  107.6 4.4 %collective-permute-done.5 = f32[3,8]{1,0:T(4,128)S(1)} collective-permute-done((f32[3,8]{1,0:T(4,128)S(1)}, f32[3,8]{1,0:T(4,128)S(1)}, u32[]{:S(2)}, u32[]{:S(2)}) %collective-permute-start.5) | collective-permute-done | bytes 128 | tf_op jit(solution)/shard_map/ppermute | solution.py:564
  112.1 0.6 slice_add_fusion
  (63 shorter events, 0.9 us)
Async XLA Ops:
  0.6 13.9 %copy-start.18 = (s32[64]{0:T(128)S(1)}, s32[64]{0:T(128)}, u32[]{:S(2)}) copy-start(s32[64]{0:T(128)} %param.22) | copy-start | bytes 772
  0.6 13.7 %copy-start.16 = (f32[256,24]{0,1:T(8,128)S(1)}, f32[256,24]{0,1:T(8,128)}, u32[]{:S(2)}) copy-start(f32[256,24]{0,1:T(8,128)} %param.28) | copy-start | bytes 73732
  0.7 13.9 %copy-start.19 = (f32[8]{0:T(128)S(1)}, f32[8]{0:T(128)}, u32[]{:S(2)}) copy-start(f32[8]{0:T(128)} %param.27) | copy-start | bytes 100
  0.7 14.5 %copy-start.6 = (f32[256,256]{1,0:T(8,128)S(1)}, f32[256,256]{1,0:T(8,128)}, u32[]{:S(2)}) copy-start(f32[256,256]{1,0:T(8,128)} %emb2.1) | copy-start | bytes 786436
  0.7 14.5 %copy-start.7 = (f32[2,64,256]{2,1,0:T(8,128)S(1)}, f32[2,64,256]{2,1,0:T(8,128)}, u32[]{:S(2)}) copy-start(f32[2,64,256]{2,1,0:T(8,128)} %env.1) | copy-start | bytes 393220
  0.7 14.5 %copy-start.4 = (f32[2,256,256]{2,1,0:T(8,128)S(1)}, f32[2,256,256]{2,1,0:T(8,128)}, u32[]{:S(2)}) copy-start(f32[2,256,256]{2,1,0:T(8,128)} %lat2.1) | copy-start | bytes 1572868
  0.7 14.5 %copy-start.8 = (f32[128,256]{1,0:T(8,128)S(1)}, f32[128,256]{1,0:T(8,128)}, u32[]{:S(2)}) copy-start(f32[128,256]{1,0:T(8,128)} %out1.1) | copy-start | bytes 393220
  3.0 22.7 %collective-permute-start = (f32[4,8]{1,0:T(4,128)S(1)}, f32[4,8]{1,0:T(4,128)S(1)}, u32[]{:S(2)}, u32[]{:S(2)}) collective-permute-start(f32[4,8]{1,0:T(4,128)S(1)} %select_reduce_fusion), channel_id=1, source_target_pairs={{0,32},{32,64},{64,96},{96,128},{128,160},{160,192},{192,224},{224... | collective-permute-start | bytes 392 | tf_op jit(solution)/shard_map/ppermute | solution.py:564
  4.5 21.2 %collective-permute-start.1 = (f32[4,8]{1,0:T(4,128)S(1)}, f32[4,8]{1,0:T(4,128)}, u32[]{:S(2)}, u32[]{:S(2)}) collective-permute-start(f32[4,8]{1,0:T(4,128)S(1)} %select_reduce_fusion), channel_id=1, source_target_pairs={{0,224},{32,0},{64,32},{96,64},{128,96},{160,128},{192,160},{224,1... | collective-permute-start | bytes 392 | tf_op jit(solution)/shard_map/ppermute | solution.py:564
  7.1 18.5 %collective-permute-start.2 = (f32[4,8]{1,0:T(4,128)S(1)}, f32[4,8]{1,0:T(4,128)}, u32[]{:S(2)}, u32[]{:S(2)}) collective-permute-start(f32[4,8]{1,0:T(4,128)S(1)} %select_reduce_fusion), channel_id=1, source_target_pairs={{0,1},{1,2},{2,3},{3,4},{4,5},{5,6},{6,7},{7,8},{8,9},{9,10},{10,1... | collective-permute-start | bytes 392 | tf_op jit(solution)/shard_map/ppermute | solution.py:564
  7.1 18.5 %collective-permute-start.3 = (f32[4,8]{1,0:T(4,128)S(1)}, f32[4,8]{1,0:T(4,128)}, u32[]{:S(2)}, u32[]{:S(2)}) collective-permute-start(f32[4,8]{1,0:T(4,128)S(1)} %select_reduce_fusion), channel_id=1, source_target_pairs={{0,31},{1,0},{2,1},{3,2},{4,3},{5,4},{6,5},{7,6},{8,7},{9,8},{10,9... | collective-permute-start | bytes 392 | tf_op jit(solution)/shard_map/ppermute | solution.py:564
  15.2 0.9 copy-start.9
  16.1 0.8 copy-start.14
  16.9 0.8 copy-start.15
  19.7 1.1 copy-start
  20.8 1.1 copy-start.1
  21.9 0.9 copy-start.2
  22.7 0.9 copy-start.3
  23.6 0.7 copy-start.5
  24.4 0.7 copy-start.10
  25.0 0.6 copy-start.12
  27.2 0.9 copy-start.11
  28.1 0.9 copy-start.13
  29.0 77.3 %copy-start.17 = (f32[64]{0:T(128)S(1)}, f32[64]{0:T(128)}, u32[]{:S(2)}) copy-start(f32[64]{0:T(128)} %select_reduce_fusion.2) | copy-start | bytes 772
  50.1 56.7 %collective-permute-start.7 = (f32[3,8]{1,0:T(4,128)S(1)}, f32[3,8]{1,0:T(4,128)S(1)}, u32[]{:S(2)}, u32[]{:S(2)}) collective-permute-start(f32[3,8]{1,0:T(4,128)S(1)} %bitcast.32), channel_id=1, source_target_pairs={{0,1},{1,2},{2,3},{3,4},{4,5},{5,6},{6,7},{7,8},{8,9},{9,10},{10,1... | collective-permute-start | bytes 296 | tf_op jit(solution)/shard_map/ppermute | solution.py:564
  50.2 56.6 %collective-permute-start.6 = (f32[3,8]{1,0:T(4,128)S(1)}, f32[3,8]{1,0:T(4,128)S(1)}, u32[]{:S(2)}, u32[]{:S(2)}) collective-permute-start(f32[3,8]{1,0:T(4,128)S(1)} %bitcast.33), channel_id=1, source_target_pairs={{0,31},{1,0},{2,1},{3,2},{4,3},{5,4},{6,5},{7,6},{8,7},{9,8},{10,9... | collective-permute-start | bytes 296 | tf_op jit(solution)/shard_map/ppermute | solution.py:564
  59.5 48.1 %collective-permute-start.4 = (f32[3,8]{1,0:T(4,128)S(1)}, f32[3,8]{1,0:T(4,128)S(1)}, u32[]{:S(2)}, u32[]{:S(2)}) collective-permute-start(f32[3,8]{1,0:T(4,128)S(1)} %bitcast.34), channel_id=1, source_target_pairs={{0,224},{32,0},{64,32},{96,64},{128,96},{160,128},{192,160},{224,1... | collective-permute-start | bytes 296 | tf_op jit(solution)/shard_map/ppermute | solution.py:564
  106.3 5.7 %collective-permute-start.5 = (f32[3,8]{1,0:T(4,128)S(1)}, f32[3,8]{1,0:T(4,128)S(1)}, u32[]{:S(2)}, u32[]{:S(2)}) collective-permute-start(f32[3,8]{1,0:T(4,128)S(1)} %bitcast.35), channel_id=1, source_target_pairs={{0,32},{32,64},{64,96},{96,128},{128,160},{160,192},{192,224},{224... | collective-permute-start | bytes 296 | tf_op jit(solution)/shard_map/ppermute | solution.py:564
